TPU v7x, 128 devices: a whole 4x4x4 slice. The times are simulated.
128 devices in a mesh: dp: 8 (over z, core), tensor: 16 (over y, x).
Axes of the slice: x: 4, y: 4, z: 4, core: 2. Of those that a mesh axis runs over, the one named last changes fastest.
Arguments:
- activations: bfloat16 [65536, 4096], P(('dp', 'tensor')), may hold values from -6 to 6
- cotangent: bfloat16 [65536, 11008], P('dp', 'tensor'), may hold values from -0.008178711 to 0.008178711
- projection: bfloat16 [4096, 512], replicated, may hold values from -0.25 to 0.25
- first_moment: float32 [512, 11008], P('dp', 'tensor'), may hold values from -0.6 to 0.6
- second_moment: float32 [512, 11008], P('dp', 'tensor'), may hold values from 0.01 to 1
- step_count: int32 [1], replicated, may hold values from 1 to 39
Outputs:
- update: bfloat16 [4096, 11008], P('dp', 'tensor')
- new_first: float32 [512, 11008], P('dp', 'tensor')
- new_second: float32 [512, 11008], P('dp', 'tensor')
All inputs are finite; a program needn't handle non-finite values.
Results may differ from a plain program's by a relative error of at most 0.0055.
Values may be sent and summed in bfloat16 or wider, within the bound.
A program may use at most 128 MiB of HBM per device.

v0:
```python
import jax
import jax.numpy as jnp
from jax import lax
from jax.sharding import PartitionSpec as P


def in_blocks(shard, dim, count):
    before, after = (shard.shape[:dim], shard.shape[dim + 1 :])
    return jnp.moveaxis(shard.reshape(*before, count, -1, *after), dim, 0)


def sum_at_owner(shard, axis, dim):
    count = lax.axis_size(axis)
    parts = lax.all_to_all(in_blocks(shard, dim, count), axis, 0, 0, tiled=True)
    return jnp.sum(parts, axis=0)


def laid_out(parts, dim):
    parts = jnp.moveaxis(parts, 0, dim)
    shape = parts.shape
    return parts.reshape(*shape[:dim], shape[dim] * shape[dim + 1], *shape[dim + 2 :])


def sent_to_all(shard, axis):
    count = lax.axis_size(axis)
    return lax.all_to_all(
        jnp.broadcast_to(shard[None], (count, *shard.shape)), axis, 0, 0, tiled=True
    )


def gather_directly(shard, axis, dim):
    return laid_out(sent_to_all(shard, axis), dim)


def per_device(activations, cotangent, projection, first_moment, second_moment, step_count):
    projected = jnp.dot(activations, projection, preferred_element_type=jnp.float32).astype(
        jnp.bfloat16
    )
    width = projection.shape[0]
    replica = lax.axis_index("dp")
    partial_grad = lax.dot_general(
        lax.all_gather(projected, "tensor", axis=0, tiled=True),
        cotangent,
        (((0,), (0,)), ((), ())),
        preferred_element_type=jnp.float32,
    )
    grad = sum_at_owner(partial_grad, "dp", 0)
    t_value = step_count[0].astype(jnp.float32)
    new_first = 0.9 * first_moment + 0.1 * grad
    new_second = 0.999 * second_moment + 0.001 * grad * grad
    first_hat = new_first / (1.0 - jnp.power(jnp.float32(0.9), t_value))
    second_hat = new_second / (1.0 - jnp.power(jnp.float32(0.999), t_value))
    normalized = (first_hat / (jnp.sqrt(second_hat) + 1e-08)).astype(jnp.bfloat16)
    whole_steps = gather_directly(normalized, "dp", 0)
    out_rows = width // lax.axis_size("dp")
    local_projection = lax.dynamic_slice_in_dim(projection, replica * out_rows, out_rows, 0)
    update = jnp.dot(local_projection, whole_steps, preferred_element_type=jnp.float32).astype(
        jnp.bfloat16
    )
    return (update, new_first, new_second)


def solution(mesh):
    in_specs = (
        P(("dp", "tensor"), None),
        P("dp", "tensor"),
        P(),
        P("dp", "tensor"),
        P("dp", "tensor"),
        P(),
    )
    out_specs = (P("dp", "tensor"), P("dp", "tensor"), P("dp", "tensor"))
    return jax.shard_map(
        per_device, mesh=mesh, in_specs=in_specs, out_specs=out_specs, check_vma=False
    )
```

profile of v0, /device:TPU:1, one launch (start us, length us, event | category | flops | bytes accessed | tf_op | source)
XLA Modules:
  0.0 154.9 jit_solution(16666026992883483268)
XLA Ops:
  7.2 0.0 all-gather.2.cloned.1.call-start
  7.2 6.6 %convolution_convert_fusion.1 = bf16[512,512]{1,0:T(8,128)(2,1)} fusion(bf16[512,4096]{1,0:T(8,128)(2,1)} %param.6, bf16[4096,512]{1,0:T(8,128)(2,1)} %param.8), kind=kOutput, calls=%fused_computation.1 | convolution fusion | flops 2147745792 | bytes 8912896 | tf_op jit(solution)/shard_map/dot_general | solution.py:36
  13.8 0.0 all-gather.2.cloned.1.call-update
  13.8 74.0 %all-gather.2.cloned.1.call-done = bf16[8192,512]{1,0:T(8,128)(2,1)} async-done(((bf16[512,512]{1,0:T(8,128)(2,1)}), bf16[8192,512]{1,0:T(8,128)(2,1)}) %all-gather.2.cloned.1.call-update) | async-done | bytes 8388624 | tf_op jit(solution)/shard_map/all_gather | solution.py:42
  87.8 13.3 %fusion.4 = f32[512,688]{1,0:T(8,128)} fusion(bf16[8192,512]{1,0:T(8,128)(2,1)} %all-gather.2.cloned.1.call-done, bf16[8192,688]{0,1:T(8,128)(2,1)} %param.7), kind=kOutput, calls=%fused_computation.8 | convolution fusion | flops 5771362304 | bytes 21069824 | tf_op jit(solution)/shard_map/dot_general | solution.py:41
  101.1 0.0 copy-start
  101.1 0.0 copy-start.1
  101.1 5.2 %all-to-all-start = ((f32[8,64,688]{2,1,0:T(8,128)}), f32[8,64,688]{2,1,0:T(8,128)S(1)}, u32[]{:S(2)}, u32[]{:S(2)}) async-start(f32[8,64,688]{2,1,0:T(8,128)} %bitcast), calls=%async_computation | async-start | bytes 3145728 | tf_op jit(solution)/shard_map/all_to_all | solution.py:14
  107.1 20.0 %all-to-all-done = f32[8,64,688]{2,1,0:T(8,128)S(1)} async-done(((f32[8,64,688]{2,1,0:T(8,128)}), f32[8,64,688]{2,1,0:T(8,128)S(1)}, u32[]{:S(2)}, u32[]{:S(2)}) %all-to-all-start) | async-done | bytes 1409056 | tf_op jit(solution)/shard_map/all_to_all | solution.py:14
  127.1 0.1 reduce_sum.9
  127.2 0.0 copy-done
  127.2 0.0 copy-done.1
  127.2 0.9 divide_convert_fusion
  128.0 0.9 broadcast_in_dim.2
  129.0 4.3 %all-to-all-start.1 = ((bf16[8,64,688]{2,1,0:T(8,128)(2,1)}), bf16[8,64,688]{2,1,0:T(8,128)(2,1)S(1)}, u32[]{:S(2)}, u32[]{:S(2)}) async-start(bf16[8,64,688]{2,1,0:T(8,128)(2,1)} %broadcast_in_dim.2), calls=%async_computation.1 | async-start | bytes 1572864 | tf_op jit(solution)/shard_map/all_to_all | solution.py:26
  133.3 12.3 %all-to-all-done.1 = bf16[8,64,688]{2,1,0:T(8,128)(2,1)S(1)} async-done(((bf16[8,64,688]{2,1,0:T(8,128)(2,1)}), bf16[8,64,688]{2,1,0:T(8,128)(2,1)S(1)}, u32[]{:S(2)}, u32[]{:S(2)}) %all-to-all-start.1) | async-done | bytes 704544 | tf_op jit(solution)/shard_map/all_to_all | solution.py:26
  145.6 2.5 %convolution_convert_fusion = bf16[512,688]{0,1:T(8,128)(2,1)} fusion(bf16[512,688]{1,0:T(8,128)(2,1)S(1)} %bitcast.9, bf16[4096,512]{1,0:T(8,128)(2,1)} %param.8, s32[]{:T(128)S(6)} %select_n.3), kind=kOutput, calls=%fused_computation | convolution fusion | flops 361062400 | bytes 1933316 | tf_op jit(solution)/shard_map/dot_general | solution.py:57
Async XLA Ops:
  7.2 80.6 %all-gather.2.cloned.1.call-start = ((), (), s32[]{:S(2)}) async-start(), calls=%async_computation.2 | async-start | bytes 8912896 | tf_op jit(solution)/shard_map/all_gather | solution.py:42
  101.1 26.0 %copy-start = (f32[64,688]{1,0:T(8,128)S(1)}, f32[64,688]{1,0:T(8,128)}, u32[]{:S(2)}) copy-start(f32[64,688]{1,0:T(8,128)} %param.10) | copy-start | bytes 528388
  101.1 26.1 %copy-start.1 = (f32[64,688]{1,0:T(8,128)S(1)}, f32[64,688]{1,0:T(8,128)}, u32[]{:S(2)}) copy-start(f32[64,688]{1,0:T(8,128)} %param.9) | copy-start | bytes 528388
  101.1 25.9 %all-to-all-start = ((f32[8,64,688]{2,1,0:T(8,128)}), f32[8,64,688]{2,1,0:T(8,128)S(1)}, u32[]{:S(2)}, u32[]{:S(2)}) async-start(f32[8,64,688]{2,1,0:T(8,128)} %bitcast), calls=%async_computation | async-start | bytes 3145728 | tf_op jit(solution)/shard_map/all_to_all | solution.py:14
  129.0 16.6 %all-to-all-start.1 = ((bf16[8,64,688]{2,1,0:T(8,128)(2,1)}), bf16[8,64,688]{2,1,0:T(8,128)(2,1)S(1)}, u32[]{:S(2)}, u32[]{:S(2)}) async-start(bf16[8,64,688]{2,1,0:T(8,128)(2,1)} %broadcast_in_dim.2), calls=%async_computation.1 | async-start | bytes 1572864 | tf_op jit(solution)/shard_map/all_to_all | solution.py:26
Sparse Core Ops, SparseCore 0:
  13.9 73.8 all-gather.1
where the time goes:
time: 155 us
  waiting for transfers between devices  106 us (68%)
  matrix products  22.4 us (14%)
  between operations  14.8 us (10%)
  starting transfers between devices  9.59 us (6%)
    all_gather x1, waiting for transfers between devices, per_device(): lax.all_gather(projected, 'tensor', axis=0, tiled=True)  74 us
    all_to_all x1, waiting for transfers between devices, sum_at_owner(): parts = lax.all_to_all(in_blocks(shard, dim, count), axis, 0, 0, tiled=True)  20 us
    dot_general x1, matrix products, per_device(): lax.dot_general(lax.all_gather(projected, 'tensor', axis=0, tiled=True),...  13.3 us
    all_to_all x1, waiting for transfers between devices, sent_to_all(): lax.all_to_all(jnp.broadcast_to(shard[None], (count, *shard.shape)), axis...  12.3 us
    dot_general x1, matrix products, per_device(): jnp.dot(activations, projection, preferred_element_type=jnp.float32)  6.59 us
    all_to_all x1, starting transfers between devices, sum_at_owner(): parts = lax.all_to_all(in_blocks(shard, dim, count), axis, 0, 0, tiled=True)  5.23 us
    all_to_all x1, starting transfers between devices, sent_to_all(): lax.all_to_all(jnp.broadcast_to(shard[None], (count, *shard.shape)), axis...  4.32 us
  transfers between devices with their start and end apart: 3, of which 3 were waited for; matrix products, arithmetic and copies ran while one was open for 0% of the time, Pallas kernels for 0%

commit v1 on v0

--- a/solution.py
+++ b/solution.py
@@ -39,7 +39,9 @@
     width = projection.shape[0]
     replica = lax.axis_index("dp")
     partial_grad = lax.dot_general(
-        lax.all_gather(projected, "tensor", axis=0, tiled=True),
+        jnp.concatenate(
+            lax.all_to_all(jnp.stack([projected] * lax.axis_size("tensor")), "tensor", 0, 0), axis=0
+        ),
         cotangent,
         (((0,), (0,)), ((), ())),
         preferred_element_type=jnp.float32,

time: 155 us -> 197 us (1.27)
  blocking collectives: 0 us -> 102 us
  waiting for transfers between devices: 106 us -> 32.3 us
  local copies, waits for them, and re-layouts: 0.94 us -> 26.2 us
  between operations: 14.8 us -> 1.41 us
  starting transfers between devices: 9.59 us -> 11.8 us
    all_to_all x0 -> x1, blocking collectives: none -> 102 us  [per_device(): lax.all_to_all(jnp.stack([projected] * lax.axis_size('tensor')), 'tensor'...]
    all_gather x1 -> x0, waiting for transfers between devices: 74 us -> none  [per_device(): lax.all_gather(projected, 'tensor', axis=0, tiled=True)]
    all_to_all x0 -> x1, local copies, waits for them, and re-layouts: none -> 12.3 us  [per_device(): lax.all_to_all(jnp.stack([projected] * lax.axis_size('tensor')), 'tensor'...]
    dot_general x0 -> x1, local copies, waits for them, and re-layouts: none -> 11.9 us  [per_device(): lax.dot_general(jnp.concatenate(lax.all_to_all(jnp.stack([projected] * la...]
    all_to_all x1, starting transfers between devices: 5.23 us -> 7.44 us  [sum_at_owner(): parts = lax.all_to_all(in_blocks(shard, dim, count), axis, 0, 0, tiled=True)]
  transfers between devices with their start and end apart: 3 -> 2, of which waited for: 3 -> 2; matrix products, arithmetic and copies ran while one was open for 0% -> 0% of each run, Pallas kernels for 0% -> 0%
where the time goes in v1:
time: 197 us; the launch traced here: 196 us
  blocking collectives  102 us (52%)
  waiting for transfers between devices  32.3 us (16%)
  local copies, waits for them, and re-layouts  26.2 us (13%)
  matrix products  21.6 us (11%)
  starting transfers between devices  11.8 us (6%)
    all_to_all x1, blocking collectives, per_device(): lax.all_to_all(jnp.stack([projected] * lax.axis_size('tensor')), 'tensor'...  102 us
    all_to_all x1, waiting for transfers between devices, sum_at_owner(): parts = lax.all_to_all(in_blocks(shard, dim, count), axis, 0, 0, tiled=True)  20 us
    dot_general x1, matrix products, per_device(): lax.dot_general(jnp.concatenate(lax.all_to_all(jnp.stack([projected] * la...  13.3 us
    all_to_all x1, local copies, waits for them, and re-layouts, per_device(): lax.all_to_all(jnp.stack([projected] * lax.axis_size('tensor')), 'tensor'...  12.3 us
    all_to_all x1, waiting for transfers between devices, sent_to_all(): lax.all_to_all(jnp.broadcast_to(shard[None], (count, *shard.shape)), axis...  12.3 us
    dot_general x1, local copies, waits for them, and re-layouts, per_device(): lax.dot_general(jnp.concatenate(lax.all_to_all(jnp.stack([projected] * la...  11.9 us
    all_to_all x1, starting transfers between devices, sum_at_owner(): parts = lax.all_to_all(in_blocks(shard, dim, count), axis, 0, 0, tiled=True)  7.44 us
    dot_general x1, matrix products, per_device(): jnp.dot(activations, projection, preferred_element_type=jnp.float32)  5.79 us
  transfers between devices with their start and end apart: 2, of which 2 were waited for; matrix products, arithmetic and copies ran while one was open for 0% of the time, Pallas kernels for 0%

profile of v1, /device:TPU:1, one launch (start us, length us, event | category | flops | bytes accessed | tf_op | source)
XLA Modules:
  0.0 196.5 jit_solution(14682324265484842137)
XLA Ops:
  0.6 5.8 %convolution_convert_fusion.1 = bf16[512,512]{1,0:T(8,128)(2,1)S(1)} fusion(bf16[512,4096]{1,0:T(8,128)(2,1)} %param.6, bf16[4096,512]{1,0:T(8,128)(2,1)} %param.8), kind=kOutput, calls=%fused_computation.3 | convolution fusion | flops 2147745792 | bytes 8912896 | tf_op jit(solution)/shard_map/dot_general | solution.py:36
  6.4 0.2 copy.11
  6.6 0.8 stack.2
  7.5 102.3 %all_to_all.15 = bf16[16,512,512]{1,2,0:T(8,128)(2,1)} all-to-all(bf16[16,512,512]{1,2,0:T(8,128)(2,1)S(1)} %stack.2), channel_id=1, replica_groups=mesh['dp'=8,'tensor'=16] {'tensor'}, dimensions={0} | all-to-all | bytes 16777216 | tf_op jit(solution)/shard_map/all_to_all | solution.py:43
  109.7 12.3 %copy.12 = bf16[16,512,512]{2,1,0:T(8,128)(2,1)} copy(bf16[16,512,512]{1,2,0:T(8,128)(2,1)} %all_to_all.15) | data formatting | bytes 16777216 | tf_op jit(solution)/shard_map/all_to_all | solution.py:43
  122.1 11.9 %copy.13 = bf16[512,8192]{1,0:T(8,128)(2,1)} copy(bf16[512,8192]{0,1:T(8,128)(2,1)} %bitcast.14) | data formatting | bytes 16777216 | tf_op jit(solution)/shard_map/dot_general | solution.py:41
  134.0 13.3 %fusion = f32[8,64,688]{2,1,0:T(8,128)} fusion(bf16[8,64,8192]{2,1,0:T(8,128)(2,1)} %bitcast.15, bf16[8192,688]{0,1:T(8,128)(2,1)} %param.7), kind=kOutput, calls=%fused_computation | convolution fusion | flops 5771362304 | bytes 21069824 | tf_op jit(solution)/shard_map/dot_general | solution.py:41
  147.3 0.0 copy-start
  147.3 0.0 copy-start.1
  147.3 7.4 %all-to-all-start.1 = ((f32[8,64,688]{2,1,0:T(8,128)}), f32[8,64,688]{2,1,0:T(8,128)S(1)}, u32[]{:S(2)}, u32[]{:S(2)}) async-start(f32[8,64,688]{2,1,0:T(8,128)} %fusion), calls=%async_computation.1 | async-start | bytes 3145728 | tf_op jit(solution)/shard_map/all_to_all | solution.py:14
  155.4 20.0 %all-to-all-done.1 = f32[8,64,688]{2,1,0:T(8,128)S(1)} async-done(((f32[8,64,688]{2,1,0:T(8,128)}), f32[8,64,688]{2,1,0:T(8,128)S(1)}, u32[]{:S(2)}, u32[]{:S(2)}) %all-to-all-start.1) | async-done | bytes 1409056 | tf_op jit(solution)/shard_map/all_to_all | solution.py:14
  175.4 0.1 reduce_sum.9
  175.5 0.0 copy-done
  175.5 0.0 copy-done.1
  175.5 0.9 divide_convert_fusion
  176.4 0.9 broadcast_in_dim.2
  177.4 4.3 %all-to-all-start.2 = ((bf16[8,64,688]{2,1,0:T(8,128)(2,1)}), bf16[8,64,688]{2,1,0:T(8,128)(2,1)S(1)}, u32[]{:S(2)}, u32[]{:S(2)}) async-start(bf16[8,64,688]{2,1,0:T(8,128)(2,1)} %broadcast_in_dim.2), calls=%async_computation.2 | async-start | bytes 1572864 | tf_op jit(solution)/shard_map/all_to_all | solution.py:26
  181.7 12.3 %all-to-all-done.2 = bf16[8,64,688]{2,1,0:T(8,128)(2,1)S(1)} async-done(((bf16[8,64,688]{2,1,0:T(8,128)(2,1)}), bf16[8,64,688]{2,1,0:T(8,128)(2,1)S(1)}, u32[]{:S(2)}, u32[]{:S(2)}) %all-to-all-start.2) | async-done | bytes 704544 | tf_op jit(solution)/shard_map/all_to_all | solution.py:26
  194.0 2.5 %convolution_convert_fusion = bf16[512,688]{0,1:T(8,128)(2,1)} fusion(bf16[512,688]{1,0:T(8,128)(2,1)S(1)} %bitcast.16, bf16[4096,512]{1,0:T(8,128)(2,1)} %param.8, s32[]{:T(128)S(6)} %select_n.3), kind=kOutput, calls=%fused_computation.2 | convolution fusion | flops 361062400 | bytes 1933316 | tf_op jit(solution)/shard_map/dot_general | solution.py:59
Async XLA Ops:
  147.3 28.3 %copy-start = (f32[64,688]{1,0:T(8,128)S(1)}, f32[64,688]{1,0:T(8,128)}, u32[]{:S(2)}) copy-start(f32[64,688]{1,0:T(8,128)} %param.10) | copy-start | bytes 528388
  147.3 28.3 %copy-start.1 = (f32[64,688]{1,0:T(8,128)S(1)}, f32[64,688]{1,0:T(8,128)}, u32[]{:S(2)}) copy-start(f32[64,688]{1,0:T(8,128)} %param.9) | copy-start | bytes 528388
  147.3 28.2 %all-to-all-start.1 = ((f32[8,64,688]{2,1,0:T(8,128)}), f32[8,64,688]{2,1,0:T(8,128)S(1)}, u32[]{:S(2)}, u32[]{:S(2)}) async-start(f32[8,64,688]{2,1,0:T(8,128)} %fusion), calls=%async_computation.1 | async-start | bytes 3145728 | tf_op jit(solution)/shard_map/all_to_all | solution.py:14
  177.4 16.6 %all-to-all-start.2 = ((bf16[8,64,688]{2,1,0:T(8,128)(2,1)}), bf16[8,64,688]{2,1,0:T(8,128)(2,1)S(1)}, u32[]{:S(2)}, u32[]{:S(2)}) async-start(bf16[8,64,688]{2,1,0:T(8,128)(2,1)} %broadcast_in_dim.2), calls=%async_computation.2 | async-start | bytes 1572864 | tf_op jit(solution)/shard_map/all_to_all | solution.py:26
